TPU v7x, 32 devices: a whole 2x2x4 slice. The times are simulated.
32 devices in a mesh: section: 2 (over core), row: 4 (over z), col: 4 (over y, x).
Axes of the slice: x: 2, y: 2, z: 4, core: 2. Of those that a mesh axis runs over, the one named last changes fastest.
Arguments:
- acts: bfloat16 [2, 4096, 768], P(None, ('row', 'col')), may hold values from -6 to 6
- segments: int32 [2, 4096], P(None, 'row'), may hold values from 0 to 2, as said below
- norm_gains: float32 [2, 2, 768], P('section'), may hold values from 0.5 to 1.5
- norm_biases: float32 [2, 2, 768], P('section'), may hold values from -1.2 to 1.2
- w_qkv: bfloat16 [2, 768, 2304], P('section', 'row', 'col'), may hold values from -0.21875 to 0.21875
- w_out: bfloat16 [2, 768, 768], P('section', 'col', 'row'), may hold values from -2 to 2
- w_up: bfloat16 [2, 768, 3072], P('section', 'row', 'col'), may hold values from -0.21875 to 0.21875
- w_down: bfloat16 [2, 3072, 768], P('section', 'col', 'row'), may hold values from -0.109375 to 0.109375
- out_grad: bfloat16 [2, 4096, 768], P(None, ('row', 'col')), may hold values from -6 to 6
Outputs:
- layer_outputs: bfloat16 [2, 2, 4096, 768], P('section', None, ('row', 'col'))
- input_grads: bfloat16 [2, 2, 4096, 768], P('section', None, ('row', 'col'))
- grad_gains: float32 [2, 2, 768], P('section')
- grad_biases: float32 [2, 768], P('section')
- grad_mlp_biases: float32 [2, 768], P('section')
- grad_qkv: float32 [2, 768, 2304], P('section', 'row', 'col')
- grad_out: float32 [2, 768, 768], P('section', 'col', 'row')
- grad_up: float32 [2, 768, 3072], P('section', 'row', 'col')
- grad_down: float32 [2, 3072, 768], P('section', 'col', 'row')
Inputs may be any that keep to these rules, and one draw needn't show every extreme that they name: `segments`: in every sequence of 1024 tokens the segment numbers start at 0, never fall and rise by one at each new document; a sequence holds one to three documents of 200 to 1024 tokens.
All inputs are finite; a program needn't handle non-finite values.
Results may differ from a plain program's by a relative error of at most 0.019.
Values may be sent and summed in bfloat16 or wider, within the bound.
A program may use at most 128 MiB of HBM per device.

v0:
```python
from functools import partial

import jax
import jax.numpy as jnp
from jax import lax
from jax.experimental import pallas as pl
from jax.experimental.pallas import tpu as pltpu
from jax.sharding import PartitionSpec as P

HD = 64
ROT = 16
EPSILON = 1e-05
F32 = jnp.float32
BF16 = jnp.bfloat16


def contract(left, right, left_dim, right_dim):
    return lax.dot_general(
        left, right, (((left_dim,), (right_dim,)), ((), ())), preferred_element_type=F32
    )


def col_gather(piece):
    n = lax.axis_size("col")
    me = lax.axis_index("col")
    rows = piece.shape[0]
    pieces = [piece]
    for k in range(1, n):
        pieces.append(lax.ppermute(piece, "col", [(i, (i + k) % n) for i in range(n)]))
    whole = jnp.zeros((rows * n, piece.shape[1]), piece.dtype)
    for k in range(n):
        whole = lax.dynamic_update_slice(whole, pieces[k], (lax.rem(me - k + n, n) * rows, 0))
    return whole


def col_scatter(total):
    n = lax.axis_size("col")
    me = lax.axis_index("col")
    rows = total.shape[0] // n
    width = total.shape[1]
    low = total.astype(BF16)

    def chunk(source, k):
        return lax.dynamic_slice(source, (lax.rem(me + k, n) * rows, 0), (rows, width))

    arrived = [
        lax.ppermute(chunk(low, k), "col", [(i, (i + k) % n) for i in range(n)])
        for k in range(1, n)
    ]
    result = chunk(total, 0)
    for piece in arrived:
        result = result + piece.astype(F32)
    return result


def remote(source, target, send, recv, device):
    return pltpu.make_async_remote_copy(
        src_ref=source,
        dst_ref=target,
        send_sem=send,
        recv_sem=recv,
        device_id=device,
        device_id_type=pl.DeviceIdType.MESH,
    )


def greet(devices):
    barrier = pltpu.get_barrier_semaphore()
    for device in devices:
        pl.semaphore_signal(
            barrier, inc=1, device_id=device, device_id_type=pl.DeviceIdType.MESH
        )
    pl.semaphore_wait(barrier, len(devices))


def opening_kernel(nr, nc, *refs):
    pieces, outs = refs[:5], refs[5:10]
    local, row_send, row_recv, pair_send, pair_recv, col_send, col_recv = refs[10:]
    section, row, col = (lax.axis_index(a) for a in ("section", "row", "col"))
    partner = {"section": 1 - section}
    rows = [{"row": lax.rem(row + k, nr)} for k in range(1, nr)]
    cols = [{"col": lax.rem(col + k, nc)} for k in range(1, nc)]
    greet(rows + cols + [partner])
    weights, wholes = pieces[:3], outs[:3]
    tokens, gathered = pieces[3:], outs[3:]
    waits = []
    for k in range(1, nr):
        for j in range(3):
            copy = remote(
                weights[j],
                wholes[j].at[section, row],
                row_send.at[j * nr + k],
                row_recv.at[j * nr + k],
                rows[k - 1],
            )
            copy.start()
            waits.append(copy)
    for k in range(1, nc):
        for j in range(2):
            copy = remote(
                tokens[j],
                gathered[j].at[col],
                col_send.at[j * nc + k],
                col_recv.at[j * nc + k],
                cols[k - 1],
            )
            copy.start()
            waits.append(copy)
    locals_here = []
    passing = []
    for j in range(3):
        locals_here.append(
            pltpu.make_async_copy(weights[j], wholes[j].at[section, row], local.at[j])
        )
        passing.append(
            remote(
                weights[j],
                wholes[j].at[section, row],
                pair_send.at[j * nr],
                pair_recv.at[j * nr],
                partner,
            )
        )
    for j in range(2):
        locals_here.append(
            pltpu.make_async_copy(tokens[j], gathered[j].at[col], local.at[3 + j])
        )
    for copy in locals_here + passing:
        copy.start()
    for k in range(1, nr):
        origin = lax.rem(row - k + nr, nr)
        for j in range(3):
            waits[(k - 1) * 3 + j].wait_recv()
            copy = remote(
                wholes[j].at[section, origin],
                wholes[j].at[section, origin],
                pair_send.at[j * nr + k],
                pair_recv.at[j * nr + k],
                partner,
            )
            copy.start()
            passing.append(copy)
    for copy in locals_here:
        copy.wait()
    for at, copy in enumerate(waits):
        copy.wait_send()
        if at >= 3 * (nr - 1):
            copy.wait_recv()
    for copy in passing:
        copy.wait()


def opening(weights, tokens):
    nr, nc = lax.axis_size("row"), lax.axis_size("col")
    shapes = [jax.ShapeDtypeStruct((2, nr) + w.shape, w.dtype) for w in weights]
    shapes += [jax.ShapeDtypeStruct((nc,) + t.shape, t.dtype) for t in tokens]
    sems = [5, 3 * nr, 3 * nr, 3 * nr, 3 * nr, 2 * nc, 2 * nc]
    return pl.pallas_call(
        partial(opening_kernel, nr, nc),
        out_shape=shapes,
        in_specs=[pl.BlockSpec(memory_space=pl.ANY)] * 5,
        out_specs=[pl.BlockSpec(memory_space=pl.ANY)] * 5,
        scratch_shapes=[pltpu.SemaphoreType.DMA((count,)) for count in sems],
        compiler_params=pltpu.CompilerParams(collective_id=0, has_side_effects=True),
        name="opening",
    )(*weights, *tokens)


def pairs_of(section, shift, n):
    return [(section * n + i, section * n + (i + shift) % n) for i in range(n)]


def row_scatter(term, axis, section):
    n = lax.axis_size("row")
    other = lax.ppermute(term.astype(BF16), "section", [(1 - section, section)])
    total = term + other.astype(F32)
    if n > 8:
        return lax.psum_scatter(
            total.astype(BF16), "row", scatter_dimension=axis, tiled=True
        ).astype(F32)
    me = lax.axis_index("row")
    sizes = tuple(d // n if a == axis else d for a, d in enumerate(term.shape))

    def chunk(k):
        at = lax.rem(me + k, n) * sizes[axis]
        return lax.dynamic_slice(total, (at, 0) if axis == 0 else (0, at), sizes)

    arrived = [
        lax.ppermute(chunk(k).astype(BF16), ("section", "row"), pairs_of(section, k, n))
        for k in range(1, n)
    ]
    result = chunk(0)
    for piece in arrived:
        result = result + piece.astype(F32)
    return result


def rotary_tables(length, heads):
    places = jnp.arange(length).astype(F32)
    inverse = 10000.0 ** (-jnp.arange(0, ROT, 2).astype(F32) / ROT)
    angles = places[:, None] * inverse[None, :]
    cosine, sine = jnp.cos(angles), jnp.sin(angles)
    half = ROT // 2
    ones = jnp.ones((length, HD - ROT), F32)
    zeros = jnp.zeros((length, HD - ROT), F32)
    nil = jnp.zeros((length, half), F32)
    cos_one = jnp.concatenate([cosine, cosine, ones], axis=1)
    ahead_one = jnp.concatenate([-sine, nil, zeros], axis=1)
    behind_one = jnp.concatenate([nil, sine, zeros], axis=1)
    flat = jnp.zeros((length, HD), F32)

    def full(one, last):
        return jnp.tile(jnp.concatenate([one, one, last], axis=1), (1, heads))

    return full(cos_one, flat + 1.0), full(ahead_one, flat), full(behind_one, flat)


def shifted(array, by):
    return jnp.roll(array, by, axis=1)


def rotate(packed, tables):
    cosine, ahead, behind = tables
    half = ROT // 2
    return packed * cosine + shifted(packed, -half) * ahead + shifted(packed, half) * behind


def rotate_back(grad, tables):
    cosine, ahead, behind = tables
    half = ROT // 2
    return grad * cosine + shifted(grad * ahead, half) + shifted(grad * behind, -half)


def scores_of(query_block, keys_all, segment, begin, stop):
    places = jnp.arange(stop)
    scores = jnp.einsum(
        "qhd,khd->hqk", query_block, keys_all[:stop], preferred_element_type=F32
    ) * HD ** (-0.5)
    allowed = (segment[begin:stop, None] == segment[None, :stop]) & (
        places[begin:, None] >= places[None, :]
    )
    return jnp.where(allowed[None], scores, -1000000000.0)


def split_heads(packed):
    length, width = packed.shape
    parts = packed.reshape(length, width // (3 * HD), 3, HD)
    return parts[:, :, 0], parts[:, :, 1], parts[:, :, 2]


def attention_forward(packed, segment):
    queries, keys_all, values = split_heads(packed)
    length = packed.shape[0]
    block = min(512, length)
    outputs, totals = [], []
    for begin in range(0, length, block):
        stop = begin + block
        scores = scores_of(queries[begin:stop], keys_all, segment, begin, stop)
        biggest = jnp.max(scores, axis=-1, keepdims=True)
        raised = jnp.exp(scores - biggest)
        summed = jnp.sum(raised, axis=-1, keepdims=True)
        softened = (raised / summed).astype(BF16)
        outputs.append(
            jnp.einsum("hqk,khd->qhd", softened, values[:stop], preferred_element_type=F32)
        )
        totals.append((biggest + jnp.log(summed))[..., 0])
    context = jnp.concatenate(outputs, axis=0).astype(BF16).reshape(length, -1)
    return context, jnp.concatenate(totals, axis=1)


def attention_backward(packed, segment, log_totals, context_grad):
    queries, keys_all, values = split_heads(packed)
    length, heads = queries.shape[:2]
    context_grad = context_grad.reshape(length, heads, HD)
    block = min(512, length)
    factor = HD ** (-0.5)
    key_grad = jnp.zeros(keys_all.shape, F32)
    value_grad = jnp.zeros(values.shape, F32)
    query_grads = []
    for begin in range(0, length, block):
        stop = begin + block
        query_block = queries[begin:stop]
        grad_block = context_grad[begin:stop]
        scores = scores_of(query_block, keys_all, segment, begin, stop)
        softened = jnp.exp(scores - log_totals[:, begin:stop, None])
        soft_grad = jnp.einsum(
            "qhd,khd->hqk", grad_block, values[:stop], preferred_element_type=F32
        )
        inner = jnp.sum(softened * soft_grad, axis=-1, keepdims=True)
        score_grad = (softened * (soft_grad - inner)).astype(BF16)
        query_grads.append(
            jnp.einsum("hqk,khd->qhd", score_grad, keys_all[:stop], preferred_element_type=F32)
            * factor
        )
        key_grad = key_grad.at[:stop].add(
            jnp.einsum("hqk,qhd->khd", score_grad, query_block, preferred_element_type=F32)
            * factor
        )
        value_grad = value_grad.at[:stop].add(
            jnp.einsum(
                "hqk,qhd->khd", softened.astype(BF16), grad_block, preferred_element_type=F32
            )
        )
    grads = jnp.stack([jnp.concatenate(query_grads, axis=0), key_grad, value_grad], axis=2)
    return grads.reshape(length, -1)


def normalize(inputs):
    values_in = inputs.astype(F32)
    centre = jnp.mean(values_in, axis=1, keepdims=True)
    spread = jnp.mean(values_in * values_in, axis=1, keepdims=True) - centre * centre
    inverse = lax.rsqrt(spread + EPSILON)
    return (values_in - centre) * inverse, inverse


def layer_forward(own, inputs, segment, weights, gains, biases, tables):
    qkv, up, both = weights
    scaled = normalize(inputs)[0]
    attn_in = (scaled * gains[0] + biases[0]).astype(BF16)
    mlp_in = (scaled * gains[1] + biases[1]).astype(BF16)
    packed = rotate(jnp.dot(attn_in, qkv, preferred_element_type=F32), tables).astype(BF16)
    context, log_totals = attention_forward(packed, segment)
    hidden = jnp.dot(mlp_in, up, preferred_element_type=F32)
    active = jax.nn.gelu(hidden, approximate=False).astype(BF16)
    joined = jnp.concatenate([context, active], axis=1)
    branch = col_scatter(jnp.dot(joined, both, preferred_element_type=F32))
    result = (own.astype(F32) + branch).astype(BF16)
    return result, (own, inputs, attn_in, mlp_in, packed, log_totals, context)


def layer_backward(own_grad, grad_all, stored, segment, weights, gains, tables):
    qkv, up, both = weights
    own, inputs, attn_in, mlp_in, packed, log_totals, context = stored
    width = context.shape[1]
    joined_grad = contract(grad_all, both, 1, 1)
    context_grad = joined_grad[:, :width].astype(BF16)
    hidden = jnp.dot(mlp_in, up, preferred_element_type=F32)
    active, gelu_pull = jax.vjp(partial(jax.nn.gelu, approximate=False), hidden)
    hidden_grad = gelu_pull(joined_grad[:, width:])[0].astype(BF16)
    packed_grad = attention_backward(packed, segment, log_totals, context_grad)
    packed_grad = rotate_back(packed_grad, tables).astype(BF16)
    attn_grad = contract(packed_grad, qkv, 1, 1)
    mlp_grad = contract(hidden_grad, up, 1, 1)
    reduced = col_scatter(attn_grad * gains[0] + mlp_grad * gains[1])
    scaled_own, inverse_own = normalize(own)
    grad_mean = jnp.mean(reduced, axis=1, keepdims=True)
    cross_mean = jnp.mean(reduced * scaled_own, axis=1, keepdims=True)
    input_grad = own_grad.astype(F32) + inverse_own * (
        reduced - grad_mean - scaled_own * cross_mean
    )
    scaled = normalize(inputs)[0]
    small = jnp.stack(
        [
            jnp.sum(attn_grad * scaled, axis=0),
            jnp.sum(mlp_grad * scaled, axis=0),
            jnp.sum(attn_grad, axis=0),
            jnp.sum(mlp_grad, axis=0),
        ]
    )
    qkv_term = contract(attn_in, packed_grad, 0, 0)
    up_term = contract(mlp_in, hidden_grad, 0, 0)
    joined = jnp.concatenate([context, active.astype(BF16)], axis=1)
    both_term = contract(joined, grad_all, 0, 0)
    return input_grad.astype(BF16), (qkv_term, up_term, both_term), small


def butterfly(value, axis):
    n = lax.axis_size(axis)
    step = 1
    while step < n:
        value = value + lax.ppermute(value, axis, [(i, i ^ step) for i in range(n)])
        step *= 2
    return value


def body(acts, segments, norm_gains, norm_biases, w_qkv, w_out, w_up, w_down, out_grad):
    section = lax.axis_index("section")
    first = section == 0

    def mine(member):
        return lax.dynamic_index_in_dim(member, section, 0, keepdims=False)

    def swap(value):
        return lax.ppermute(value, "section", [(0, 1), (1, 0)])

    own = mine(acts)
    segment = mine(segments)
    last_grad = mine(out_grad)
    joined_local = jnp.concatenate([w_out[0], w_down[0]], axis=0)
    qkv_all, up_all, both_all, inputs, grad_all = opening(
        (w_qkv[0], w_up[0], joined_local), (own, last_grad)
    )
    width = own.shape[1]
    inputs, grad_all = inputs.reshape(-1, width), grad_all.reshape(-1, width)
    weights = [
        (
            qkv_all[layer].reshape(width, -1),
            up_all[layer].reshape(width, -1),
            both_all[layer].transpose(1, 0, 2).reshape(-1, width),
        )
        for layer in range(2)
    ]
    norms = jnp.concatenate([norm_gains[0], norm_biases[0]], axis=0)
    norms_other = swap(norms)
    layer_norms = [
        jnp.where(first, norms, norms_other),
        jnp.where(first, norms_other, norms),
    ]
    gains = [member[:2] for member in layer_norms]
    biases = [member[2:] for member in layer_norms]
    tables = rotary_tables(inputs.shape[0], w_qkv.shape[2] // (3 * HD))

    middle, stored_first = layer_forward(
        own, inputs, segment, weights[0], gains[0], biases[0], tables
    )
    inputs_last = col_gather(middle)
    last, stored_last = layer_forward(
        middle, inputs_last, segment, weights[1], gains[1], biases[1], tables
    )
    middle_grad, terms_last, small_last = layer_backward(
        last_grad, grad_all, stored_last, segment, weights[1], gains[1], tables
    )
    middle_grad_all = col_gather(middle_grad)
    totals_last = [row_scatter(t, a, 1) for t, a in zip(terms_last, (0, 0, 1))]
    first_grad, terms_first, small_first = layer_backward(
        middle_grad, middle_grad_all, stored_first, segment, weights[0], gains[0], tables
    )
    totals_first = [row_scatter(t, a, 0) for t, a in zip(terms_first, (0, 0, 1))]
    totals = [jnp.where(first, a, b) for a, b in zip(totals_first, totals_last)]

    small = jnp.where(first, small_first, small_last) + swap(
        jnp.where(first, small_last, small_first)
    )
    small = butterfly(butterfly(small, "col"), "row")

    def placed(of_first, of_last):
        kept = jnp.where(first, of_first, of_last)
        arrived = swap(jnp.where(first, of_last, of_first))
        return jnp.where(first, jnp.stack([kept, arrived]), jnp.stack([arrived, kept]))[None]

    split = w_out.shape[1]
    return (
        placed(middle, last),
        placed(first_grad, middle_grad),
        small[:2][None],
        small[2][None],
        small[3][None],
        totals[0][None],
        totals[2][:split][None],
        totals[1][None],
        totals[2][split:][None],
    )


def solution(mesh):
    placed = (
        P(None, ("row", "col"), None),
        P(None, "row"),
        P("section", None, None),
        P("section", None, None),
        P("section", "row", "col"),
        P("section", "col", "row"),
        P("section", "row", "col"),
        P("section", "col", "row"),
        P(None, ("row", "col"), None),
    )
    return jax.shard_map(
        body,
        mesh=mesh,
        in_specs=placed,
        out_specs=(
            P("section", None, ("row", "col"), None),
            P("section", None, ("row", "col"), None),
            P("section", None, None),
            P("section", None),
            P("section", None),
            P("section", "row", "col"),
            P("section", "col", "row"),
            P("section", "row", "col"),
            P("section", "col", "row"),
        ),
        check_vma=False,
    )
```

profile of v0, /device:TPU:11, one launch (start us, length us, event | category | flops | bytes accessed | tf_op | source)
XLA Modules:
  0.0 483.6 jit_solution(5523664825932557284)
XLA Ops:
  9.2 95.4 %opening.1 = (bf16[2,4,192,576]{3,2,1,0:T(8,128)(2,1)}, bf16[2,4,192,768]{3,2,1,0:T(8,128)(2,1)}, bf16[2,4,960,192]{3,2,1,0:T(8,128)(2,1)}, bf16[4,256,768]{2,1,0:T(8,128)(2,1)}, bf16[4,256,768]{2,1,0:T(8,128)(2,1)}) custom-call(bf16[192,576]{1,0:T(8,128)(2,1)} %bitcast.386, bf16[192,768]{1,0:T(8,128)(2,1)} %bitcast.385, ...), custom_call_target="tpu_custom_call" | custom-call | tf_op jit(solution)/shard_map/opening/pallas_call | solution.py:158
  118.1 3.8 copy.67
  121.9 5.5 %fusion.172 = (bf16[1024,960]{0,1:T(8,128)(2,1)S(1)}, f32[1024,960]{0,1:T(8,128)}) fusion(bf16[1024,768]{1,0:T(8,128)(2,1)} %bitcast.398, bf16[960,768]{0,1:T(8,128)(2,1)} %bitcast.365), kind=kOutput, calls=%fused_computation.374 | convolution fusion | flops 1510932480 | bytes 8945664 | tf_op jit(solution)/shard_map/dot_general | solution.py:18
  130.0 4.0 copy.57
  150.4 9.6 %multiply_convert_fusion.5 = (bf16[1024,768]{0,1:T(8,128)(2,1)S(1)}, f32[1024,768]{0,1:T(8,128)}, f32[1024,768]{0,1:T(8,128)}) fusion(bf16[1024,768]{1,0:T(8,128)(2,1)S(1)} %bitcast.371, bf16[768,768]{1,0:T(8,128)(2,1)S(1)} %bitcast.376), kind=kOutput, calls=%fused_computation.81 | convolution fusion | flops 1259077632 | bytes 10616832 | tf_op jit(solution)/shard_map/dot_general | solution.py:323
  164.8 7.9 %collective-permute-done.1 = bf16[256,768]{1,0:T(8,128)(2,1)S(1)} collective-permute-done((bf16[256,768]{1,0:T(8,128)(2,1)S(1)}, bf16[256,768]{1,0:T(8,128)(2,1)S(1)}, u32[]{:S(2)}, u32[]{:S(2)}) %collective-permute-start.1) | collective-permute-done | bytes 393248 | tf_op jit(solution)/shard_map/ppermute | solution.py:47
  173.6 8.5 %collective-permute-done.3 = bf16[256,768]{1,0:T(8,128)(2,1)S(1)} collective-permute-done((bf16[256,768]{1,0:T(8,128)(2,1)S(1)}, bf16[256,768]{1,0:T(8,128)(2,1)S(1)}, u32[]{:S(2)}, u32[]{:S(2)}) %collective-permute-start.3) | collective-permute-done | bytes 393248 | tf_op jit(solution)/shard_map/ppermute | solution.py:47
  185.7 6.5 %collective-permute-done.4 = bf16[256,768]{1,0:T(8,128)(2,1)S(1)} collective-permute-done((bf16[256,768]{1,0:T(8,128)(2,1)S(1)}, bf16[256,768]{1,0:T(8,128)(2,1)S(1)}, u32[]{:S(2)}, u32[]{:S(2)}) %collective-permute-start.4) | collective-permute-done | bytes 393248 | tf_op jit(solution)/shard_map/ppermute | solution.py:29
  192.2 3.4 collective-permute-done.5
  195.7 5.4 %collective-permute-done.6 = bf16[256,768]{1,0:T(8,128)(2,1)S(1)} collective-permute-done((bf16[256,768]{1,0:T(8,128)(2,1)S(1)}, bf16[256,768]{1,0:T(8,128)(2,1)S(1)}, u32[]{:S(2)}, u32[]{:S(2)}) %collective-permute-start.6) | collective-permute-done | bytes 393248 | tf_op jit(solution)/shard_map/ppermute | solution.py:29
  225.2 9.0 %add_convert_fusion.2 = (bf16[1024,768]{0,1:T(8,128)(2,1)S(1)}, f32[1024,768]{0,1:T(8,128)S(1)}, f32[1024,768]{0,1:T(8,128)S(1)}) fusion(f32[1024,960]{0,1:T(8,128)S(1)} %copy-done.58, bf16[768,768]{1,0:T(8,128)(2,1)S(1)} %bitcast.378, bf16[1024,768]{1,0:T(8,128)(2,1)S(1)} %constant_dynamic-update-slice_fusion.10, f32[768]{0:T(1024)S(1)} %get-tuple-element.190, ...), kind=kOutput, calls=%fused_computation.60 | convolution fusion | flops 1269301248 | bytes 13776896 | tf_op jit(solution)/shard_map/dot_general | solution.py:323
  241.9 3.5 fusion.175
  260.7 4.1 collective-permute-done.11
  269.3 4.2 collective-permute-done.13
  275.3 6.6 %collective-permute-done.9 = bf16[256,768]{1,0:T(8,128)(2,1)S(1)} collective-permute-done((bf16[256,768]{1,0:T(8,128)(2,1)S(1)}, bf16[256,768]{1,0:T(8,128)(2,1)S(1)}, u32[]{:S(2)}, u32[]{:S(2)}) %collective-permute-start.9) | collective-permute-done | bytes 393248 | tf_op jit(solution)/shard_map/ppermute | solution.py:47
  284.9 5.3 %collective-permute-start.14 = (bf16[256,768]{1,0:T(8,128)(2,1)S(1)}, bf16[256,768]{1,0:T(8,128)(2,1)S(1)}, u32[]{:S(2)}, u32[]{:S(2)}) collective-permute-start(bf16[256,768]{1,0:T(8,128)(2,1)S(1)} %get-tuple-element.204), channel_id=1, source_target_pairs={{0,1},{1,2},{2,3},{3,0},{4,5},{5,6},{6,7},{7,4},{8,9},{9,10},{10,1... | collective-permute-start | bytes 1179656 | tf_op jit(solution)/shard_map/ppermute | solution.py:29
  297.5 4.0 collective-permute-done.15
  301.6 8.6 %collective-permute-start.10 = (bf16[256,768]{1,0:T(8,128)(2,1)}, bf16[256,768]{1,0:T(8,128)(2,1)}, u32[]{:S(2)}, u32[]{:S(2)}) collective-permute-start(bf16[256,768]{1,0:T(8,128)(2,1)} %get-tuple-element.277), channel_id=1, source_target_pairs={{0,16},{16,0},{1,17},{17,1},{2,18},{18,2},{3,19},{19,3},{4,20},{20... | collective-permute-start | bytes 1179656 | tf_op jit(solution)/shard_map/ppermute | solution.py:384
  344.1 4.6 collective-permute-start.25
  355.0 7.0 %collective-permute-start.42 = (bf16[768,768]{1,0:T(8,128)(2,1)S(1)}, bf16[768,768]{1,0:T(8,128)(2,1)S(1)}, u32[]{:S(2)}, u32[]{:S(2)}) collective-permute-start(bf16[768,768]{1,0:T(8,128)(2,1)S(1)} %get-tuple-element.335), channel_id=1, source_target_pairs={{16,0},{17,1},{18,2},{19,3},{20,4},{21,5},{22,6},{23,7},{24,8},{25... | collective-permute-start | bytes 3538952 | tf_op jit(solution)/shard_map/ppermute | solution.py:175
  362.0 5.8 %collective-permute-done.18 = bf16[256,768]{1,0:T(8,128)(2,1)S(1)} collective-permute-done((bf16[256,768]{1,0:T(8,128)(2,1)S(1)}, bf16[256,768]{1,0:T(8,128)(2,1)S(1)}, u32[]{:S(2)}, u32[]{:S(2)}) %collective-permute-start.18) | collective-permute-done | bytes 393248 | tf_op jit(solution)/shard_map/ppermute | solution.py:47
  367.8 5.1 %collective-permute-start.34 = (bf16[960,768]{1,0:T(8,128)(2,1)S(1)}, bf16[960,768]{1,0:T(8,128)(2,1)S(1)}, u32[]{:S(2)}, u32[]{:S(2)}) collective-permute-start(bf16[960,768]{1,0:T(8,128)(2,1)S(1)} %get-tuple-element.331), channel_id=1, source_target_pairs={{16,0},{17,1},{18,2},{19,3},{20,4},{21,5},{22,6},{23,7},{24,8},{25... | collective-permute-start | bytes 4423688 | tf_op jit(solution)/shard_map/ppermute | solution.py:175
  383.8 3.9 collective-permute-start.32
  394.6 5.1 %collective-permute-done.32 = bf16[192,576]{0,1:T(8,128)(2,1)S(1)} collective-permute-done((bf16[192,576]{0,1:T(8,128)(2,1)S(1)}, bf16[192,576]{0,1:T(8,128)(2,1)S(1)}, u32[]{:S(2)}, u32[]{:S(2)}) %collective-permute-start.32) | collective-permute-done | bytes 221216 | tf_op jit(solution)/shard_map/ppermute | solution.py:189
  399.7 4.7 collective-permute-start.48
  404.4 8.3 %collective-permute-done.33 = bf16[192,576]{0,1:T(8,128)(2,1)S(1)} collective-permute-done((bf16[192,576]{0,1:T(8,128)(2,1)S(1)}, bf16[192,576]{0,1:T(8,128)(2,1)S(1)}, u32[]{:S(2)}, u32[]{:S(2)}) %collective-permute-start.33) | collective-permute-done | bytes 221216 | tf_op jit(solution)/shard_map/ppermute | solution.py:189
  414.6 4.0 collective-permute-done.47
  418.6 3.8 collective-permute-start.39
  423.6 7.7 %collective-permute-done.48 = bf16[192,768]{1,0:T(8,128)(2,1)S(1)} collective-permute-done((bf16[192,768]{1,0:T(8,128)(2,1)S(1)}, bf16[192,768]{1,0:T(8,128)(2,1)S(1)}, u32[]{:S(2)}, u32[]{:S(2)}) %collective-permute-start.48) | collective-permute-done | bytes 294944 | tf_op jit(solution)/shard_map/ppermute | solution.py:189
  432.0 10.6 %collective-permute-done.49 = bf16[192,768]{1,0:T(8,128)(2,1)S(1)} collective-permute-done((bf16[192,768]{1,0:T(8,128)(2,1)S(1)}, bf16[192,768]{1,0:T(8,128)(2,1)S(1)}, u32[]{:S(2)}, u32[]{:S(2)}) %collective-permute-start.49) | collective-permute-done | bytes 294944 | tf_op jit(solution)/shard_map/ppermute | solution.py:189
  450.9 3.9 collective-permute-start.41
  463.5 14.7 %collective-permute-done.40 = bf16[960,192]{1,0:T(8,128)(2,1)} collective-permute-done((bf16[960,192]{1,0:T(8,128)(2,1)}, bf16[960,192]{1,0:T(8,128)(2,1)}, u32[]{:S(2)}, u32[]{:S(2)}) %collective-permute-start.40) | collective-permute-done | bytes 368672 | tf_op jit(solution)/shard_map/ppermute | solution.py:189
  (394 shorter events, 196.0 us)
Async XLA Ops:
  2.0 132.1 %collective-permute-start = (f32[4,768]{1,0:T(4,128)}, f32[4,768]{1,0:T(4,128)}, u32[]{:S(2)}, u32[]{:S(2)}) collective-permute-start(f32[4,768]{1,0:T(4,128)} %pad_maximum_fusion.13), channel_id=1, source_target_pairs={{0,16},{16,0},{1,17},{17,1},{2,18},{18,2},{3,19},{19,3},{4,20},{20... | collective-permute-start | bytes 36872 | tf_op jit(solution)/shard_map/ppermute | solution.py:384
  164.4 17.6 %collective-permute-start.3 = (bf16[256,768]{1,0:T(8,128)(2,1)S(1)}, bf16[256,768]{1,0:T(8,128)(2,1)S(1)}, u32[]{:S(2)}, u32[]{:S(2)}) collective-permute-start(bf16[256,768]{1,0:T(8,128)(2,1)S(1)} %get-tuple-element.275), channel_id=1, source_target_pairs={{0,3},{1,0},{2,1},{3,2},{4,7},{5,4},{6,5},{7,6},{8,11},{9,8},{10,9... | collective-permute-start | bytes 1179656 | tf_op jit(solution)/shard_map/ppermute | solution.py:47
  184.3 16.8 %collective-permute-start.6 = (bf16[256,768]{1,0:T(8,128)(2,1)S(1)}, bf16[256,768]{1,0:T(8,128)(2,1)S(1)}, u32[]{:S(2)}, u32[]{:S(2)}) collective-permute-start(bf16[256,768]{1,0:T(8,128)(2,1)S(1)} %get-tuple-element.206), channel_id=1, source_target_pairs={{0,3},{1,0},{2,1},{3,2},{4,7},{5,4},{6,5},{7,6},{8,11},{9,8},{10,9... | collective-permute-start | bytes 1179656 | tf_op jit(solution)/shard_map/ppermute | solution.py:29
  245.5 29.8 %collective-permute-start.7 = (bf16[256,768]{1,0:T(8,128)(2,1)S(1)}, bf16[256,768]{1,0:T(8,128)(2,1)}, u32[]{:S(2)}, u32[]{:S(2)}) collective-permute-start(bf16[256,768]{1,0:T(8,128)(2,1)S(1)} %get-tuple-element.271), channel_id=1, source_target_pairs={{0,1},{1,2},{2,3},{3,0},{4,5},{5,6},{6,7},{7,4},{8,9},{9,10},{10,1... | collective-permute-start | bytes 1179656 | tf_op jit(solution)/shard_map/ppermute | solution.py:47
  248.6 26.7 %collective-permute-start.8 = (bf16[256,768]{1,0:T(8,128)(2,1)S(1)}, bf16[256,768]{1,0:T(8,128)(2,1)}, u32[]{:S(2)}, u32[]{:S(2)}) collective-permute-start(bf16[256,768]{1,0:T(8,128)(2,1)S(1)} %get-tuple-element.273), channel_id=1, source_target_pairs={{0,2},{1,3},{2,0},{3,1},{4,6},{5,7},{6,4},{7,5},{8,10},{9,11},{10,... | collective-permute-start | bytes 1179656 | tf_op jit(solution)/shard_map/ppermute | solution.py:47
  255.0 13.1 %collective-permute-start.12 = (bf16[256,768]{1,0:T(8,128)(2,1)S(1)}, bf16[256,768]{1,0:T(8,128)(2,1)S(1)}, u32[]{:S(2)}, u32[]{:S(2)}) collective-permute-start(bf16[256,768]{1,0:T(8,128)(2,1)S(1)} %get-tuple-element.270), channel_id=1, source_target_pairs={{0,2},{1,3},{2,0},{3,1},{4,6},{5,7},{6,4},{7,5},{8,10},{9,11},{10,... | collective-permute-start | bytes 1179656 | tf_op jit(solution)/shard_map/ppermute | solution.py:47
  256.1 17.5 %collective-permute-start.13 = (bf16[256,768]{1,0:T(8,128)(2,1)S(1)}, bf16[256,768]{1,0:T(8,128)(2,1)S(1)}, u32[]{:S(2)}, u32[]{:S(2)}) collective-permute-start(bf16[256,768]{1,0:T(8,128)(2,1)S(1)} %get-tuple-element.269), channel_id=1, source_target_pairs={{0,3},{1,0},{2,1},{3,2},{4,7},{5,4},{6,5},{7,6},{8,11},{9,8},{10,9... | collective-permute-start | bytes 1179656 | tf_op jit(solution)/shard_map/ppermute | solution.py:47
  264.7 17.2 %collective-permute-start.9 = (bf16[256,768]{1,0:T(8,128)(2,1)S(1)}, bf16[256,768]{1,0:T(8,128)(2,1)S(1)}, u32[]{:S(2)}, u32[]{:S(2)}) collective-permute-start(bf16[256,768]{1,0:T(8,128)(2,1)S(1)} %get-tuple-element.272), channel_id=1, source_target_pairs={{0,3},{1,0},{2,1},{3,2},{4,7},{5,4},{6,5},{7,6},{8,11},{9,8},{10,9... | collective-permute-start | bytes 1179656 | tf_op jit(solution)/shard_map/ppermute | solution.py:47
  268.1 107.1 %collective-permute-start.46 = (bf16[768,768]{1,0:T(8,128)(2,1)}, bf16[768,768]{1,0:T(8,128)(2,1)S(1)}, u32[]{:S(2)}, u32[]{:S(2)}) collective-permute-start(bf16[768,768]{1,0:T(8,128)(2,1)} %get-tuple-element.333), channel_id=1, source_target_pairs={{0,16},{1,17},{2,18},{3,19},{4,20},{5,21},{6,22},{7,23},{8,24},{9,... | collective-permute-start | bytes 3538952 | tf_op jit(solution)/shard_map/ppermute | solution.py:175
  273.5 106.9 %collective-permute-start.38 = (bf16[960,768]{1,0:T(8,128)(2,1)}, bf16[960,768]{1,0:T(8,128)(2,1)}, u32[]{:S(2)}, u32[]{:S(2)}) collective-permute-start(bf16[960,768]{1,0:T(8,128)(2,1)} %get-tuple-element.329), channel_id=1, source_target_pairs={{0,16},{1,17},{2,18},{3,19},{4,20},{5,21},{6,22},{7,23},{8,24},{9,... | collective-permute-start | bytes 4423688 | tf_op jit(solution)/shard_map/ppermute | solution.py:175
  290.6 19.6 %collective-permute-start.16 = (bf16[256,768]{1,0:T(8,128)(2,1)S(1)}, bf16[256,768]{1,0:T(8,128)(2,1)S(1)}, u32[]{:S(2)}, u32[]{:S(2)}) collective-permute-start(bf16[256,768]{1,0:T(8,128)(2,1)S(1)} %get-tuple-element.204), channel_id=1, source_target_pairs={{0,3},{1,0},{2,1},{3,2},{4,7},{5,4},{6,5},{7,6},{8,11},{9,8},{10,9... | collective-permute-start | bytes 1179656 | tf_op jit(solution)/shard_map/ppermute | solution.py:29
  296.2 56.3 %collective-permute-start.30 = (bf16[768,576]{0,1:T(8,128)(2,1)}, bf16[768,576]{0,1:T(8,128)(2,1)}, u32[]{:S(2)}, u32[]{:S(2)}) collective-permute-start(bf16[768,576]{0,1:T(8,128)(2,1)} %get-tuple-element.325), channel_id=1, source_target_pairs={{0,16},{1,17},{2,18},{3,19},{4,20},{5,21},{6,22},{7,23},{8,24},{9,... | collective-permute-start | bytes 2654216 | tf_op jit(solution)/shard_map/ppermute | solution.py:175
  301.6 42.5 %collective-permute-start.10 = (bf16[256,768]{1,0:T(8,128)(2,1)}, bf16[256,768]{1,0:T(8,128)(2,1)}, u32[]{:S(2)}, u32[]{:S(2)}) collective-permute-start(bf16[256,768]{1,0:T(8,128)(2,1)} %get-tuple-element.277), channel_id=1, source_target_pairs={{0,16},{16,0},{1,17},{17,1},{2,18},{18,2},{3,19},{19,3},{4,20},{20... | collective-permute-start | bytes 1179656 | tf_op jit(solution)/shard_map/ppermute | solution.py:384
  350.8 16.9 %collective-permute-start.18 = (bf16[256,768]{1,0:T(8,128)(2,1)S(1)}, bf16[256,768]{1,0:T(8,128)(2,1)S(1)}, u32[]{:S(2)}, u32[]{:S(2)}) collective-permute-start(bf16[256,768]{1,0:T(8,128)(2,1)S(1)} %get-tuple-element.267), channel_id=1, source_target_pairs={{0,2},{1,3},{2,0},{3,1},{4,6},{5,7},{6,4},{7,5},{8,10},{9,11},{10,... | collective-permute-start | bytes 1179656 | tf_op jit(solution)/shard_map/ppermute | solution.py:47
  352.5 20.3 %collective-permute-start.19 = (bf16[256,768]{1,0:T(8,128)(2,1)S(1)}, bf16[256,768]{1,0:T(8,128)(2,1)S(1)}, u32[]{:S(2)}, u32[]{:S(2)}) collective-permute-start(bf16[256,768]{1,0:T(8,128)(2,1)S(1)} %get-tuple-element.266), channel_id=1, source_target_pairs={{0,3},{1,0},{2,1},{3,2},{4,7},{5,4},{6,5},{7,6},{8,11},{9,8},{10,9... | collective-permute-start | bytes 1179656 | tf_op jit(solution)/shard_map/ppermute | solution.py:47
  355.0 67.5 %collective-permute-start.42 = (bf16[768,768]{1,0:T(8,128)(2,1)S(1)}, bf16[768,768]{1,0:T(8,128)(2,1)S(1)}, u32[]{:S(2)}, u32[]{:S(2)}) collective-permute-start(bf16[768,768]{1,0:T(8,128)(2,1)S(1)} %get-tuple-element.335), channel_id=1, source_target_pairs={{16,0},{17,1},{18,2},{19,3},{20,4},{21,5},{22,6},{23,7},{24,8},{25... | collective-permute-start | bytes 3538952 | tf_op jit(solution)/shard_map/ppermute | solution.py:175
  367.8 76.9 %collective-permute-start.34 = (bf16[960,768]{1,0:T(8,128)(2,1)S(1)}, bf16[960,768]{1,0:T(8,128)(2,1)S(1)}, u32[]{:S(2)}, u32[]{:S(2)}) collective-permute-start(bf16[960,768]{1,0:T(8,128)(2,1)S(1)} %get-tuple-element.331), channel_id=1, source_target_pairs={{16,0},{17,1},{18,2},{19,3},{20,4},{21,5},{22,6},{23,7},{24,8},{25... | collective-permute-start | bytes 4423688 | tf_op jit(solution)/shard_map/ppermute | solution.py:175
  372.9 18.4 %collective-permute-start.26 = (bf16[768,576]{0,1:T(8,128)(2,1)S(1)}, bf16[768,576]{0,1:T(8,128)(2,1)S(1)}, u32[]{:S(2)}, u32[]{:S(2)}) collective-permute-start(bf16[768,576]{0,1:T(8,128)(2,1)S(1)} %get-tuple-element.327), channel_id=1, source_target_pairs={{16,0},{17,1},{18,2},{19,3},{20,4},{21,5},{22,6},{23,7},{24,8},{25... | collective-permute-start | bytes 2654216 | tf_op jit(solution)/shard_map/ppermute | solution.py:175
  375.2 13.5 %collective-permute-start.31 = (bf16[192,576]{0,1:T(8,128)(2,1)S(1)}, bf16[192,576]{0,1:T(8,128)(2,1)S(1)}, u32[]{:S(2)}, u32[]{:S(2)}) collective-permute-start(bf16[192,576]{0,1:T(8,128)(2,1)S(1)} %get-tuple-element.259), channel_id=1, source_target_pairs={{16,20},{20,24},{24,28},{28,16},{17,21},{21,25},{25,29},{29,17},{1... | collective-permute-start | bytes 663560 | tf_op jit(solution)/shard_map/ppermute | solution.py:189
  383.8 15.9 %collective-permute-start.32 = (bf16[192,576]{0,1:T(8,128)(2,1)S(1)}, bf16[192,576]{0,1:T(8,128)(2,1)S(1)}, u32[]{:S(2)}, u32[]{:S(2)}) collective-permute-start(bf16[192,576]{0,1:T(8,128)(2,1)S(1)} %get-tuple-element.261), channel_id=1, source_target_pairs={{16,24},{20,28},{24,16},{28,20},{17,25},{21,29},{25,17},{29,21},{1... | collective-permute-start | bytes 663560 | tf_op jit(solution)/shard_map/ppermute | solution.py:189
  388.7 24.0 %collective-permute-start.33 = (bf16[192,576]{0,1:T(8,128)(2,1)S(1)}, bf16[192,576]{0,1:T(8,128)(2,1)S(1)}, u32[]{:S(2)}, u32[]{:S(2)}) collective-permute-start(bf16[192,576]{0,1:T(8,128)(2,1)S(1)} %get-tuple-element.260), channel_id=1, source_target_pairs={{16,28},{20,16},{24,20},{28,24},{17,29},{21,17},{25,21},{29,25},{1... | collective-permute-start | bytes 663560 | tf_op jit(solution)/shard_map/ppermute | solution.py:189
  391.3 27.4 %collective-permute-start.47 = (bf16[192,768]{1,0:T(8,128)(2,1)S(1)}, bf16[192,768]{1,0:T(8,128)(2,1)S(1)}, u32[]{:S(2)}, u32[]{:S(2)}) collective-permute-start(bf16[192,768]{1,0:T(8,128)(2,1)S(1)} %get-tuple-element.230), channel_id=1, source_target_pairs={{16,20},{20,24},{24,28},{28,16},{17,21},{21,25},{25,29},{29,17},{1... | collective-permute-start | bytes 884744 | tf_op jit(solution)/shard_map/ppermute | solution.py:189
  399.7 31.6 %collective-permute-start.48 = (bf16[192,768]{1,0:T(8,128)(2,1)S(1)}, bf16[192,768]{1,0:T(8,128)(2,1)S(1)}, u32[]{:S(2)}, u32[]{:S(2)}) collective-permute-start(bf16[192,768]{1,0:T(8,128)(2,1)S(1)} %get-tuple-element.232), channel_id=1, source_target_pairs={{16,24},{20,28},{24,16},{28,20},{17,25},{21,29},{25,17},{29,21},{1... | collective-permute-start | bytes 884744 | tf_op jit(solution)/shard_map/ppermute | solution.py:189
  412.7 29.9 %collective-permute-start.49 = (bf16[192,768]{1,0:T(8,128)(2,1)S(1)}, bf16[192,768]{1,0:T(8,128)(2,1)S(1)}, u32[]{:S(2)}, u32[]{:S(2)}) collective-permute-start(bf16[192,768]{1,0:T(8,128)(2,1)S(1)} %get-tuple-element.231), channel_id=1, source_target_pairs={{16,28},{20,16},{24,20},{28,24},{17,29},{21,17},{25,21},{29,25},{1... | collective-permute-start | bytes 884744 | tf_op jit(solution)/shard_map/ppermute | solution.py:189
  418.6 24.6 %collective-permute-start.39 = (bf16[960,192]{1,0:T(8,128)(2,1)S(1)}, bf16[960,192]{1,0:T(8,128)(2,1)S(1)}, u32[]{:S(2)}, u32[]{:S(2)}) collective-permute-start(bf16[960,192]{1,0:T(8,128)(2,1)S(1)} %get-tuple-element.224), channel_id=1, source_target_pairs={{16,20},{20,24},{24,28},{28,16},{17,21},{21,25},{25,29},{29,17},{1... | collective-permute-start | bytes 1105928 | tf_op jit(solution)/shard_map/ppermute | solution.py:189
  422.5 21.5 %collective-permute-start.27 = (bf16[192,576]{0,1:T(8,128)(2,1)S(1)}, bf16[192,576]{0,1:T(8,128)(2,1)S(1)}, u32[]{:S(2)}, u32[]{:S(2)}) collective-permute-start(bf16[192,576]{0,1:T(8,128)(2,1)S(1)} %get-tuple-element.256), channel_id=1, source_target_pairs={{0,4},{4,8},{8,12},{12,0},{1,5},{5,9},{9,13},{13,1},{2,6},{6,10},{... | collective-permute-start | bytes 663560 | tf_op jit(solution)/shard_map/ppermute | solution.py:189
  431.3 17.6 %collective-permute-start.28 = (bf16[192,576]{0,1:T(8,128)(2,1)S(1)}, bf16[192,576]{0,1:T(8,128)(2,1)S(1)}, u32[]{:S(2)}, u32[]{:S(2)}) collective-permute-start(bf16[192,576]{0,1:T(8,128)(2,1)S(1)} %get-tuple-element.258), channel_id=1, source_target_pairs={{0,8},{4,12},{8,0},{12,4},{1,9},{5,13},{9,1},{13,5},{2,10},{6,14},... | collective-permute-start | bytes 663560 | tf_op jit(solution)/shard_map/ppermute | solution.py:189
  448.9 29.3 %collective-permute-start.40 = (bf16[960,192]{1,0:T(8,128)(2,1)}, bf16[960,192]{1,0:T(8,128)(2,1)}, u32[]{:S(2)}, u32[]{:S(2)}) collective-permute-start(bf16[960,192]{1,0:T(8,128)(2,1)} %get-tuple-element.226), channel_id=1, source_target_pairs={{16,24},{20,28},{24,16},{28,20},{17,25},{21,29},{25,17},{29,21},{1... | collective-permute-start | bytes 1105928 | tf_op jit(solution)/shard_map/ppermute | solution.py:189
  450.9 27.8 %collective-permute-start.41 = (bf16[960,192]{1,0:T(8,128)(2,1)}, bf16[960,192]{1,0:T(8,128)(2,1)}, u32[]{:S(2)}, u32[]{:S(2)}) collective-permute-start(bf16[960,192]{1,0:T(8,128)(2,1)} %get-tuple-element.225), channel_id=1, source_target_pairs={{16,28},{20,16},{24,20},{28,24},{17,29},{21,17},{25,21},{29,25},{1... | collective-permute-start | bytes 1105928 | tf_op jit(solution)/shard_map/ppermute | solution.py:189
  454.8 23.9 %collective-permute-start.35 = (bf16[960,192]{1,0:T(8,128)(2,1)}, bf16[960,192]{1,0:T(8,128)(2,1)}, u32[]{:S(2)}, u32[]{:S(2)}) collective-permute-start(bf16[960,192]{1,0:T(8,128)(2,1)} %get-tuple-element.221), channel_id=1, source_target_pairs={{0,4},{4,8},{8,12},{12,0},{1,5},{5,9},{9,13},{13,1},{2,6},{6,10},{... | collective-permute-start | bytes 1105928 | tf_op jit(solution)/shard_map/ppermute | solution.py:189
  456.3 22.4 %collective-permute-start.36 = (bf16[960,192]{1,0:T(8,128)(2,1)}, bf16[960,192]{1,0:T(8,128)(2,1)}, u32[]{:S(2)}, u32[]{:S(2)}) collective-permute-start(bf16[960,192]{1,0:T(8,128)(2,1)} %get-tuple-element.223), channel_id=1, source_target_pairs={{0,8},{4,12},{8,0},{12,4},{1,9},{5,13},{9,1},{13,5},{2,10},{6,14},... | collective-permute-start | bytes 1105928 | tf_op jit(solution)/shard_map/ppermute | solution.py:189
  457.7 21.0 %collective-permute-start.37 = (bf16[960,192]{1,0:T(8,128)(2,1)}, bf16[960,192]{1,0:T(8,128)(2,1)}, u32[]{:S(2)}, u32[]{:S(2)}) collective-permute-start(bf16[960,192]{1,0:T(8,128)(2,1)} %get-tuple-element.222), channel_id=1, source_target_pairs={{0,12},{4,0},{8,4},{12,8},{1,13},{5,1},{9,5},{13,9},{2,14},{6,2},{... | collective-permute-start | bytes 1105928 | tf_op jit(solution)/shard_map/ppermute | solution.py:189
  (82 other events, 561.0 us)
where the time goes:
time: 490 us; the launch traced here: 484 us
  waiting for transfers between devices  117 us (24%)
  Pallas kernels  95.4 us (19%)
  starting transfers between devices  89.9 us (18%)
  matrix products  79.4 us (16%)
  other arithmetic  53.2 us (11%)
  local copies, waits for them, and re-layouts  46.1 us (9%)
    pallas_call x1, Pallas kernels, opening(): pl.pallas_call(partial(opening_kernel, nr, nc), out_shape=shapes, in_spec...  95.4 us
    ppermute x18, waiting for transfers between devices, row_scatter(): lax.ppermute(chunk(k).astype(BF16), ('section', 'row'), pairs_of(section,...  50.9 us
    ppermute x12, waiting for transfers between devices, col_scatter(): lax.ppermute(chunk(low, k), 'col', [(i, (i + k) % n) for i in range(n)])  38.9 us
    ppermute x18, starting transfers between devices, row_scatter(): lax.ppermute(chunk(k).astype(BF16), ('section', 'row'), pairs_of(section,...  35.8 us
    dot_general x12, matrix products, contract(): lax.dot_general(left, right, (((left_dim,), (right_dim,)), ((), ())), pre...  29.7 us
    ppermute x6, waiting for transfers between devices, col_gather(): lax.ppermute(piece, 'col', [(i, (i + k) % n) for i in range(n)])  22.6 us
    dot_general x2, matrix products, layer_forward(): hidden = jnp.dot(mlp_in, up, preferred_element_type=F32)  18.6 us
    ppermute x6, starting transfers between devices, row_scatter(): other = lax.ppermute(term.astype(BF16), 'section', [(1 - section, section)])  17.3 us
  transfers between devices with their start and end apart: 50, of which 23 were waited for; matrix products, arithmetic and copies ran while one was open for 20% of the time, Pallas kernels for 20%

commit v1 on v0

--- a/solution.py
+++ b/solution.py
@@ -166,33 +166,49 @@
     )(*weights, *tokens)
 
 
-def pairs_of(section, shift, n):
-    return [(section * n + i, section * n + (i + shift) % n) for i in range(n)]
-
-
-def row_scatter(term, axis, section):
-    n = lax.axis_size("row")
-    other = lax.ppermute(term.astype(BF16), "section", [(1 - section, section)])
-    total = term + other.astype(F32)
-    if n > 8:
-        return lax.psum_scatter(
-            total.astype(BF16), "row", scatter_dimension=axis, tiled=True
-        ).astype(F32)
-    me = lax.axis_index("row")
-    sizes = tuple(d // n if a == axis else d for a, d in enumerate(term.shape))
-
-    def chunk(k):
-        at = lax.rem(me + k, n) * sizes[axis]
-        return lax.dynamic_slice(total, (at, 0) if axis == 0 else (0, at), sizes)
-
-    arrived = [
-        lax.ppermute(chunk(k).astype(BF16), ("section", "row"), pairs_of(section, k, n))
-        for k in range(1, n)
+def closing_kernel(nr, *refs):
+    pieces, outs, send, recv = refs[:4], refs[4:8], refs[8], refs[9]
+    row = lax.axis_index("row")
+    targets = [lax.rem(row + k, nr) for k in range(1, nr)]
+    greet([{"row": target} for target in targets])
+    copies = []
+    for k in range(1, nr):
+        target = targets[k - 1]
+        for j in range(4):
+            copy = remote(
+                pieces[j] if j == 3 else pieces[j].at[target],
+                outs[j].at[k - 1],
+                send.at[j * nr + k],
+                recv.at[j * nr + k],
+                {"row": target},
+            )
+            copy.start()
+            copies.append(copy)
+    for copy in copies:
+        copy.wait()
+
+
+def closing(totals, small):
+    nr = lax.axis_size("row")
+    row = lax.axis_index("row")
+    low = [total.astype(BF16) for total in totals]
+    shapes = [jax.ShapeDtypeStruct((nr - 1,) + t.shape[1:], BF16) for t in low]
+    shapes.append(jax.ShapeDtypeStruct((nr - 1,) + small.shape, F32))
+    arrived = pl.pallas_call(
+        partial(closing_kernel, nr),
+        out_shape=shapes,
+        in_specs=[pl.BlockSpec(memory_space=pl.ANY)] * 4,
+        out_specs=[pl.BlockSpec(memory_space=pl.ANY)] * 4,
+        scratch_shapes=[pltpu.SemaphoreType.DMA((4 * nr,)) for _ in range(2)],
+        compiler_params=pltpu.CompilerParams(collective_id=1, has_side_effects=True),
+        name="closing",
+    )(*low, small)
+    results = [
+        lax.dynamic_index_in_dim(total, row, 0, keepdims=False)
+        + jnp.sum(pieces.astype(F32), axis=0)
+        for total, pieces in zip(totals, arrived)
     ]
-    result = chunk(0)
-    for piece in arrived:
-        result = result + piece.astype(F32)
-    return result
+    return results, small + jnp.sum(arrived[3], axis=0)
 
 
 def rotary_tables(length, heads):
@@ -421,17 +437,33 @@
         last_grad, grad_all, stored_last, segment, weights[1], gains[1], tables
     )
     middle_grad_all = col_gather(middle_grad)
-    totals_last = [row_scatter(t, a, 1) for t, a in zip(terms_last, (0, 0, 1))]
+    nr = lax.axis_size("row")
+
+    def to_section(terms, layer):
+        return [lax.ppermute(t.astype(BF16), "section", [(1 - layer, layer)]) for t in terms]
+
+    others_last = to_section(terms_last, 1)
     first_grad, terms_first, small_first = layer_backward(
         middle_grad, middle_grad_all, stored_first, segment, weights[0], gains[0], tables
     )
-    totals_first = [row_scatter(t, a, 0) for t, a in zip(terms_first, (0, 0, 1))]
-    totals = [jnp.where(first, a, b) for a, b in zip(totals_first, totals_last)]
-
+    others_first = to_section(terms_first, 0)
     small = jnp.where(first, small_first, small_last) + swap(
         jnp.where(first, small_last, small_first)
     )
-    small = butterfly(butterfly(small, "col"), "row")
+    small = butterfly(small, "col")
+    totals = [
+        jnp.where(first, a, b) + jnp.where(first, c, d).astype(F32)
+        for a, b, c, d in zip(terms_first, terms_last, others_first, others_last)
+    ]
+    qkv_total, up_total, both_total = totals
+    totals, small = closing(
+        (
+            qkv_total.reshape(nr, -1, qkv_total.shape[1]),
+            up_total.reshape(nr, -1, up_total.shape[1]),
+            both_total.reshape(both_total.shape[0], nr, -1).transpose(1, 0, 2),
+        ),
+        small,
+    )
 
     def placed(of_first, of_last):
         kept = jnp.where(first, of_first, of_last)

time: 490 us -> 521 us (1.063)
  Pallas kernels: 95.4 us -> 190 us
  starting transfers between devices: 89.9 us -> 45.1 us
  waiting for transfers between devices: 117 us -> 74.2 us
  other arithmetic: 53.2 us -> 65 us
  matrix products: 79.4 us -> 86.4 us
    pallas_call x0 -> x1, Pallas kernels: none -> 94.9 us  [closing(): pl.pallas_call(partial(closing_kernel, nr), out_shape=shapes, in_specs=[p...]
    ppermute x24 -> x6, waiting for transfers between devices: 50.9 us -> 0.02 us  [to_section(): lax.ppermute(t.astype(BF16), 'section', [(1 - layer, layer)])]
    ppermute x24 -> x6, starting transfers between devices: 53.1 us -> 14.5 us  [to_section(): lax.ppermute(t.astype(BF16), 'section', [(1 - layer, layer)])]
    ppermute x4 -> x2, waiting for transfers between devices: 4.34 us -> 14.5 us  [butterfly(): value = value + lax.ppermute(value, axis, [(i, i ^ step) for i in range(n)])]
    add x6 -> x7, other arithmetic: 5.7 us -> 13.5 us  [the longest x3 8.36 us: body(): jnp.where(first, a, b) + jnp.where(first, c, d).astype(F32)]
    dot_general x12, matrix products: 29.7 us -> 36.7 us  [contract(): lax.dot_general(left, right, (((left_dim,), (right_dim,)), ((), ())), pre...]
    ppermute x12, waiting for transfers between devices: 38.9 us -> 33.2 us  [col_scatter(): lax.ppermute(chunk(low, k), 'col', [(i, (i + k) % n) for i in range(n)])]
    unnamed x142 -> x137, local copies, waits for them, and re-layouts: 15.5 us -> 15.8 us
  transfers between devices with their start and end apart: 50 -> 30, of which waited for: 23 -> 13; matrix products, arithmetic and copies ran while one was open for 20% -> 19% of each run, Pallas kernels for 20% -> 19%
where the time goes in v1:
time: 521 us; the launch traced here: 515 us
  Pallas kernels  190 us (36%)
  matrix products  86.4 us (17%)
  waiting for transfers between devices  74.2 us (14%)
  other arithmetic  65 us (12%)
  local copies, waits for them, and re-layouts  51 us (10%)
  starting transfers between devices  45.1 us (9%)
    pallas_call x1, Pallas kernels, opening(): pl.pallas_call(partial(opening_kernel, nr, nc), out_shape=shapes, in_spec...  95.4 us
    pallas_call x1, Pallas kernels, closing(): pl.pallas_call(partial(closing_kernel, nr), out_shape=shapes, in_specs=[p...  94.9 us
    dot_general x12, matrix products, contract(): lax.dot_general(left, right, (((left_dim,), (right_dim,)), ((), ())), pre...  36.7 us
    ppermute x12, waiting for transfers between devices, col_scatter(): lax.ppermute(chunk(low, k), 'col', [(i, (i + k) % n) for i in range(n)])  33.2 us
    ppermute x6, waiting for transfers between devices, col_gather(): lax.ppermute(piece, 'col', [(i, (i + k) % n) for i in range(n)])  26.5 us
    dot_general x2, matrix products, layer_forward(): hidden = jnp.dot(mlp_in, up, preferred_element_type=F32)  18.5 us
    unnamed x137, local copies, waits for them, and re-layouts  15.8 us
    ppermute x2, waiting for transfers between devices, butterfly(): value = value + lax.ppermute(value, axis, [(i, i ^ step) for i in range(n)])  14.5 us
  transfers between devices with their start and end apart: 30, of which 13 were waited for; matrix products, arithmetic and copies ran while one was open for 19% of the time, Pallas kernels for 19%

profile of v1, /device:TPU:11, one launch (start us, length us, event | category | flops | bytes accessed | tf_op | source)
XLA Modules:
  0.0 514.6 jit_solution(17996501943224099262)
XLA Ops:
  9.2 95.4 %opening.1 = (bf16[2,4,192,576]{3,2,1,0:T(8,128)(2,1)}, bf16[2,4,192,768]{3,2,1,0:T(8,128)(2,1)}, bf16[2,4,960,192]{3,2,1,0:T(8,128)(2,1)}, bf16[4,256,768]{2,1,0:T(8,128)(2,1)}, bf16[4,256,768]{2,1,0:T(8,128)(2,1)}) custom-call(bf16[192,576]{1,0:T(8,128)(2,1)} %bitcast.399, bf16[192,768]{1,0:T(8,128)(2,1)} %bitcast.398, ...), custom_call_target="tpu_custom_call" | custom-call | tf_op jit(solution)/shard_map/opening/pallas_call | solution.py:158
  106.5 3.0 fusion.167
  112.8 3.2 fusion.162
  118.1 3.8 copy.141
  121.9 5.6 %fusion.172 = (bf16[1024,960]{0,1:T(8,128)(2,1)S(1)}, f32[1024,960]{0,1:T(8,128)}) fusion(bf16[1024,768]{1,0:T(8,128)(2,1)} %bitcast.411, bf16[960,768]{0,1:T(8,128)(2,1)} %bitcast.380), kind=kOutput, calls=%fused_computation.356 | convolution fusion | flops 1510932480 | bytes 8945664 | tf_op jit(solution)/shard_map/dot_general | solution.py:18
  130.0 3.9 copy.131
  150.3 9.5 %multiply_convert_fusion.5 = (bf16[1024,768]{0,1:T(8,128)(2,1)S(1)}, f32[1024,768]{0,1:T(8,128)}, f32[1024,768]{0,1:T(8,128)}) fusion(bf16[1024,768]{1,0:T(8,128)(2,1)S(1)} %bitcast.384, bf16[768,768]{1,0:T(8,128)(2,1)S(1)} %bitcast.389), kind=kOutput, calls=%fused_computation.81 | convolution fusion | flops 1259077632 | bytes 10616832 | tf_op jit(solution)/shard_map/dot_general | solution.py:339
  164.6 7.9 %collective-permute-done.1 = bf16[256,768]{1,0:T(8,128)(2,1)S(1)} collective-permute-done((bf16[256,768]{1,0:T(8,128)(2,1)S(1)}, bf16[256,768]{1,0:T(8,128)(2,1)S(1)}, u32[]{:S(2)}, u32[]{:S(2)}) %collective-permute-start.1) | collective-permute-done | bytes 393248 | tf_op jit(solution)/shard_map/ppermute | solution.py:47
  173.4 8.5 %collective-permute-done.3 = bf16[256,768]{1,0:T(8,128)(2,1)S(1)} collective-permute-done((bf16[256,768]{1,0:T(8,128)(2,1)S(1)}, bf16[256,768]{1,0:T(8,128)(2,1)S(1)}, u32[]{:S(2)}, u32[]{:S(2)}) %collective-permute-start.3) | collective-permute-done | bytes 393248 | tf_op jit(solution)/shard_map/ppermute | solution.py:47
  185.5 6.5 %collective-permute-done.4 = bf16[256,768]{1,0:T(8,128)(2,1)S(1)} collective-permute-done((bf16[256,768]{1,0:T(8,128)(2,1)S(1)}, bf16[256,768]{1,0:T(8,128)(2,1)S(1)}, u32[]{:S(2)}, u32[]{:S(2)}) %collective-permute-start.4) | collective-permute-done | bytes 393248 | tf_op jit(solution)/shard_map/ppermute | solution.py:29
  192.0 3.4 collective-permute-done.5
  195.5 5.4 %collective-permute-done.6 = bf16[256,768]{1,0:T(8,128)(2,1)S(1)} collective-permute-done((bf16[256,768]{1,0:T(8,128)(2,1)S(1)}, bf16[256,768]{1,0:T(8,128)(2,1)S(1)}, u32[]{:S(2)}, u32[]{:S(2)}) %collective-permute-start.6) | collective-permute-done | bytes 393248 | tf_op jit(solution)/shard_map/ppermute | solution.py:29
  224.7 9.0 %add_convert_fusion.2 = (bf16[1024,768]{0,1:T(8,128)(2,1)S(1)}, f32[1024,768]{0,1:T(8,128)S(1)}, f32[1024,768]{0,1:T(8,128)S(1)}) fusion(f32[1024,960]{0,1:T(8,128)S(1)} %copy-done.56, bf16[768,768]{1,0:T(8,128)(2,1)S(1)} %bitcast.391, bf16[1024,768]{1,0:T(8,128)(2,1)S(1)} %constant_dynamic-update-slice_fusion.10, f32[768]{0:T(1024)S(1)} %get-tuple-element.198, ...), kind=kOutput, calls=%fused_computation.60 | convolution fusion | flops 1269301248 | bytes 13776896 | tf_op jit(solution)/shard_map/dot_general | solution.py:339
  233.7 3.2 fusion.184
  236.9 3.7 fusion.180
  242.0 3.6 fusion.175
  245.7 3.1 collective-permute-start.7
  258.4 3.8 fusion.182
  268.6 5.5 %collective-permute-done.13 = bf16[256,768]{1,0:T(8,128)(2,1)S(1)} collective-permute-done((bf16[256,768]{1,0:T(8,128)(2,1)S(1)}, bf16[256,768]{1,0:T(8,128)(2,1)S(1)}, u32[]{:S(2)}, u32[]{:S(2)}) %collective-permute-start.13) | collective-permute-done | bytes 393248 | tf_op jit(solution)/shard_map/ppermute | solution.py:47
  274.6 7.9 %collective-permute-done.9 = bf16[256,768]{1,0:T(8,128)(2,1)S(1)} collective-permute-done((bf16[256,768]{1,0:T(8,128)(2,1)S(1)}, bf16[256,768]{1,0:T(8,128)(2,1)S(1)}, u32[]{:S(2)}, u32[]{:S(2)}) %collective-permute-start.9) | collective-permute-done | bytes 393248 | tf_op jit(solution)/shard_map/ppermute | solution.py:47
  285.2 3.8 collective-permute-start.14
  295.1 5.0 collective-permute-done.15
  300.2 3.4 collective-permute-done.16
  326.2 3.3 fusion.179
  329.6 5.6 %collective-permute-start.21 = (f32[4,768]{1,0:T(4,128)S(1)}, f32[4,768]{1,0:T(4,128)S(1)}, u32[]{:S(2)}, u32[]{:S(2)}) collective-permute-start(f32[4,768]{1,0:T(4,128)S(1)} %broadcast_select_fusion.2), channel_id=1, source_target_pairs={{0,16},{16,0},{1,17},{17,1},{2,18},{18,2},{3,19},{19,3},{4,20},{20... | collective-permute-start | bytes 36872 | tf_op jit(solution)/shard_map/ppermute | solution.py:400
  340.4 14.5 %collective-permute-done.22 = f32[4,768]{1,0:T(4,128)S(1)} collective-permute-done((f32[4,768]{1,0:T(4,128)S(1)}, f32[4,768]{1,0:T(4,128)S(1)}, u32[]{:S(2)}, u32[]{:S(2)}) %collective-permute-start.22) | collective-permute-done | bytes 12320 | tf_op jit(solution)/shard_map/ppermute | solution.py:387
  358.3 2.9 collective-permute-start.26
  365.6 3.8 fusion.181
  370.9 5.3 %collective-permute-start.28 = (bf16[960,768]{1,0:T(8,128)(2,1)}, bf16[960,768]{1,0:T(8,128)(2,1)}, u32[]{:S(2)}, u32[]{:S(2)}) collective-permute-start(bf16[960,768]{1,0:T(8,128)(2,1)} %get-tuple-element.323), channel_id=1, source_target_pairs={{16,0},{17,1},{18,2},{19,3},{20,4},{21,5},{22,6},{23,7},{24,8},{25... | collective-permute-start | bytes 4423688 | tf_op jit(solution)/shard_map/ppermute | solution.py:443
  394.6 3.7 convert_add_fusion
  402.1 3.7 copy.158
  405.8 94.9 %closing.1 = (bf16[3,192,576]{2,1,0:T(8,128)(2,1)}, bf16[3,192,768]{2,1,0:T(8,128)(2,1)}, bf16[3,960,192]{2,1,0:T(8,128)(2,1)}, f32[3,4,768]{2,1,0:T(4,128)}) custom-call(bf16[4,192,576]{2,1,0:T(8,128)(2,1)} %convert_element_type.356.refs_0_, bf16[4,192,768]{2,1,0:T(8,128)(2,1)} %convert_element_type.361.refs_1_, bf16[4,960,192]{2,1,0:T(8,128)(2,1)} %bitcast.349, ...), custom_call_target="tpu_custom_call" | custom-call | tf_op jit(solution)/shard_map/closing/pallas_call | solution.py:197
  (352 shorter events, 166.3 us)
Async XLA Ops:
  2.0 132.0 %collective-permute-start = (f32[4,768]{1,0:T(4,128)}, f32[4,768]{1,0:T(4,128)}, u32[]{:S(2)}, u32[]{:S(2)}) collective-permute-start(f32[4,768]{1,0:T(4,128)} %pad_maximum_fusion.13), channel_id=1, source_target_pairs={{0,16},{16,0},{1,17},{17,1},{2,18},{18,2},{3,19},{19,3},{4,20},{20... | collective-permute-start | bytes 36872 | tf_op jit(solution)/shard_map/ppermute | solution.py:400
  161.9 10.6 %collective-permute-start.1 = (bf16[256,768]{1,0:T(8,128)(2,1)S(1)}, bf16[256,768]{1,0:T(8,128)(2,1)S(1)}, u32[]{:S(2)}, u32[]{:S(2)}) collective-permute-start(bf16[256,768]{1,0:T(8,128)(2,1)S(1)} %get-tuple-element.264), channel_id=1, source_target_pairs={{0,1},{1,2},{2,3},{3,0},{4,5},{5,6},{6,7},{7,4},{8,9},{9,10},{10,1... | collective-permute-start | bytes 1179656 | tf_op jit(solution)/shard_map/ppermute | solution.py:47
  163.1 10.3 %collective-permute-start.2 = (bf16[256,768]{1,0:T(8,128)(2,1)S(1)}, bf16[256,768]{1,0:T(8,128)(2,1)S(1)}, u32[]{:S(2)}, u32[]{:S(2)}) collective-permute-start(bf16[256,768]{1,0:T(8,128)(2,1)S(1)} %get-tuple-element.266), channel_id=1, source_target_pairs={{0,2},{1,3},{2,0},{3,1},{4,6},{5,7},{6,4},{7,5},{8,10},{9,11},{10,... | collective-permute-start | bytes 1179656 | tf_op jit(solution)/shard_map/ppermute | solution.py:47
  164.2 17.6 %collective-permute-start.3 = (bf16[256,768]{1,0:T(8,128)(2,1)S(1)}, bf16[256,768]{1,0:T(8,128)(2,1)S(1)}, u32[]{:S(2)}, u32[]{:S(2)}) collective-permute-start(bf16[256,768]{1,0:T(8,128)(2,1)S(1)} %get-tuple-element.265), channel_id=1, source_target_pairs={{0,3},{1,0},{2,1},{3,2},{4,7},{5,4},{6,5},{7,6},{8,11},{9,8},{10,9... | collective-permute-start | bytes 1179656 | tf_op jit(solution)/shard_map/ppermute | solution.py:47
  182.3 9.7 %collective-permute-start.4 = (bf16[256,768]{1,0:T(8,128)(2,1)S(1)}, bf16[256,768]{1,0:T(8,128)(2,1)S(1)}, u32[]{:S(2)}, u32[]{:S(2)}) collective-permute-start(bf16[256,768]{1,0:T(8,128)(2,1)S(1)} %get-tuple-element.214), channel_id=1, source_target_pairs={{0,1},{1,2},{2,3},{3,0},{4,5},{5,6},{6,7},{7,4},{8,9},{9,10},{10,1... | collective-permute-start | bytes 1179656 | tf_op jit(solution)/shard_map/ppermute | solution.py:29
  184.0 11.4 %collective-permute-start.5 = (bf16[256,768]{1,0:T(8,128)(2,1)S(1)}, bf16[256,768]{1,0:T(8,128)(2,1)S(1)}, u32[]{:S(2)}, u32[]{:S(2)}) collective-permute-start(bf16[256,768]{1,0:T(8,128)(2,1)S(1)} %get-tuple-element.214), channel_id=1, source_target_pairs={{0,2},{1,3},{2,0},{3,1},{4,6},{5,7},{6,4},{7,5},{8,10},{9,11},{10,... | collective-permute-start | bytes 1179656 | tf_op jit(solution)/shard_map/ppermute | solution.py:29
  184.1 16.8 %collective-permute-start.6 = (bf16[256,768]{1,0:T(8,128)(2,1)S(1)}, bf16[256,768]{1,0:T(8,128)(2,1)S(1)}, u32[]{:S(2)}, u32[]{:S(2)}) collective-permute-start(bf16[256,768]{1,0:T(8,128)(2,1)S(1)} %get-tuple-element.214), channel_id=1, source_target_pairs={{0,3},{1,0},{2,1},{3,2},{4,7},{5,4},{6,5},{7,6},{8,11},{9,8},{10,9... | collective-permute-start | bytes 1179656 | tf_op jit(solution)/shard_map/ppermute | solution.py:29
  245.7 28.9 %collective-permute-start.7 = (bf16[256,768]{1,0:T(8,128)(2,1)S(1)}, bf16[256,768]{1,0:T(8,128)(2,1)S(1)}, u32[]{:S(2)}, u32[]{:S(2)}) collective-permute-start(bf16[256,768]{1,0:T(8,128)(2,1)S(1)} %get-tuple-element.261), channel_id=1, source_target_pairs={{0,1},{1,2},{2,3},{3,0},{4,5},{5,6},{6,7},{7,4},{8,9},{9,10},{10,1... | collective-permute-start | bytes 1179656 | tf_op jit(solution)/shard_map/ppermute | solution.py:47
  248.8 25.8 %collective-permute-start.8 = (bf16[256,768]{1,0:T(8,128)(2,1)S(1)}, bf16[256,768]{1,0:T(8,128)(2,1)S(1)}, u32[]{:S(2)}, u32[]{:S(2)}) collective-permute-start(bf16[256,768]{1,0:T(8,128)(2,1)S(1)} %get-tuple-element.263), channel_id=1, source_target_pairs={{0,2},{1,3},{2,0},{3,1},{4,6},{5,7},{6,4},{7,5},{8,10},{9,11},{10,... | collective-permute-start | bytes 1179656 | tf_op jit(solution)/shard_map/ppermute | solution.py:47
  255.4 9.3 %collective-permute-start.11 = (bf16[256,768]{1,0:T(8,128)(2,1)S(1)}, bf16[256,768]{1,0:T(8,128)(2,1)S(1)}, u32[]{:S(2)}, u32[]{:S(2)}) collective-permute-start(bf16[256,768]{1,0:T(8,128)(2,1)S(1)} %get-tuple-element.258), channel_id=1, source_target_pairs={{0,1},{1,2},{2,3},{3,0},{4,5},{5,6},{6,7},{7,4},{8,9},{9,10},{10,1... | collective-permute-start | bytes 1179656 | tf_op jit(solution)/shard_map/ppermute | solution.py:47
  255.5 11.7 %collective-permute-start.12 = (bf16[256,768]{1,0:T(8,128)(2,1)S(1)}, bf16[256,768]{1,0:T(8,128)(2,1)S(1)}, u32[]{:S(2)}, u32[]{:S(2)}) collective-permute-start(bf16[256,768]{1,0:T(8,128)(2,1)S(1)} %get-tuple-element.260), channel_id=1, source_target_pairs={{0,2},{1,3},{2,0},{3,1},{4,6},{5,7},{6,4},{7,5},{8,10},{9,11},{10,... | collective-permute-start | bytes 1179656 | tf_op jit(solution)/shard_map/ppermute | solution.py:47
  256.6 17.4 %collective-permute-start.13 = (bf16[256,768]{1,0:T(8,128)(2,1)S(1)}, bf16[256,768]{1,0:T(8,128)(2,1)S(1)}, u32[]{:S(2)}, u32[]{:S(2)}) collective-permute-start(bf16[256,768]{1,0:T(8,128)(2,1)S(1)} %get-tuple-element.259), channel_id=1, source_target_pairs={{0,3},{1,0},{2,1},{3,2},{4,7},{5,4},{6,5},{7,6},{8,11},{9,8},{10,9... | collective-permute-start | bytes 1179656 | tf_op jit(solution)/shard_map/ppermute | solution.py:47
  264.7 17.8 %collective-permute-start.9 = (bf16[256,768]{1,0:T(8,128)(2,1)S(1)}, bf16[256,768]{1,0:T(8,128)(2,1)S(1)}, u32[]{:S(2)}, u32[]{:S(2)}) collective-permute-start(bf16[256,768]{1,0:T(8,128)(2,1)S(1)} %get-tuple-element.262), channel_id=1, source_target_pairs={{0,3},{1,0},{2,1},{3,2},{4,7},{5,4},{6,5},{7,6},{8,11},{9,8},{10,9... | collective-permute-start | bytes 1179656 | tf_op jit(solution)/shard_map/ppermute | solution.py:47
  267.3 120.7 %collective-permute-start.27 = (bf16[768,768]{1,0:T(8,128)(2,1)}, bf16[768,768]{1,0:T(8,128)(2,1)}, u32[]{:S(2)}, u32[]{:S(2)}) collective-permute-start(bf16[768,768]{1,0:T(8,128)(2,1)} %get-tuple-element.321), channel_id=1, source_target_pairs={{0,16},{1,17},{2,18},{3,19},{4,20},{5,21},{6,22},{7,23},{8,24},{9,... | collective-permute-start | bytes 3538952 | tf_op jit(solution)/shard_map/ppermute | solution.py:443
  285.2 9.8 %collective-permute-start.14 = (bf16[256,768]{1,0:T(8,128)(2,1)S(1)}, bf16[256,768]{1,0:T(8,128)(2,1)S(1)}, u32[]{:S(2)}, u32[]{:S(2)}) collective-permute-start(bf16[256,768]{1,0:T(8,128)(2,1)S(1)} %get-tuple-element.212), channel_id=1, source_target_pairs={{0,1},{1,2},{2,3},{3,0},{4,5},{5,6},{6,7},{7,4},{8,9},{9,10},{10,1... | collective-permute-start | bytes 1179656 | tf_op jit(solution)/shard_map/ppermute | solution.py:29
  289.0 11.1 %collective-permute-start.15 = (bf16[256,768]{1,0:T(8,128)(2,1)S(1)}, bf16[256,768]{1,0:T(8,128)(2,1)S(1)}, u32[]{:S(2)}, u32[]{:S(2)}) collective-permute-start(bf16[256,768]{1,0:T(8,128)(2,1)S(1)} %get-tuple-element.212), channel_id=1, source_target_pairs={{0,2},{1,3},{2,0},{3,1},{4,6},{5,7},{6,4},{7,5},{8,10},{9,11},{10,... | collective-permute-start | bytes 1179656 | tf_op jit(solution)/shard_map/ppermute | solution.py:29
  289.4 14.2 %collective-permute-start.16 = (bf16[256,768]{1,0:T(8,128)(2,1)S(1)}, bf16[256,768]{1,0:T(8,128)(2,1)S(1)}, u32[]{:S(2)}, u32[]{:S(2)}) collective-permute-start(bf16[256,768]{1,0:T(8,128)(2,1)S(1)} %get-tuple-element.212), channel_id=1, source_target_pairs={{0,3},{1,0},{2,1},{3,2},{4,7},{5,4},{6,5},{7,6},{8,11},{9,8},{10,9... | collective-permute-start | bytes 1179656 | tf_op jit(solution)/shard_map/ppermute | solution.py:29
  329.6 7.7 %collective-permute-start.21 = (f32[4,768]{1,0:T(4,128)S(1)}, f32[4,768]{1,0:T(4,128)S(1)}, u32[]{:S(2)}, u32[]{:S(2)}) collective-permute-start(f32[4,768]{1,0:T(4,128)S(1)} %broadcast_select_fusion.2), channel_id=1, source_target_pairs={{0,16},{16,0},{1,17},{17,1},{2,18},{18,2},{3,19},{19,3},{4,20},{20... | collective-permute-start | bytes 36872 | tf_op jit(solution)/shard_map/ppermute | solution.py:400
  335.2 21.0 %collective-permute-start.17 = (bf16[256,768]{1,0:T(8,128)(2,1)S(1)}, bf16[256,768]{1,0:T(8,128)(2,1)S(1)}, u32[]{:S(2)}, u32[]{:S(2)}) collective-permute-start(bf16[256,768]{1,0:T(8,128)(2,1)S(1)} %get-tuple-element.255), channel_id=1, source_target_pairs={{0,1},{1,2},{2,3},{3,0},{4,5},{5,6},{6,7},{7,4},{8,9},{9,10},{10,1... | collective-permute-start | bytes 1179656 | tf_op jit(solution)/shard_map/ppermute | solution.py:47
  335.5 22.8 %collective-permute-start.18 = (bf16[256,768]{1,0:T(8,128)(2,1)S(1)}, bf16[256,768]{1,0:T(8,128)(2,1)S(1)}, u32[]{:S(2)}, u32[]{:S(2)}) collective-permute-start(bf16[256,768]{1,0:T(8,128)(2,1)S(1)} %get-tuple-element.257), channel_id=1, source_target_pairs={{0,2},{1,3},{2,0},{3,1},{4,6},{5,7},{6,4},{7,5},{8,10},{9,11},{10,... | collective-permute-start | bytes 1179656 | tf_op jit(solution)/shard_map/ppermute | solution.py:47
  336.6 24.6 %collective-permute-start.19 = (bf16[256,768]{1,0:T(8,128)(2,1)S(1)}, bf16[256,768]{1,0:T(8,128)(2,1)S(1)}, u32[]{:S(2)}, u32[]{:S(2)}) collective-permute-start(bf16[256,768]{1,0:T(8,128)(2,1)S(1)} %get-tuple-element.256), channel_id=1, source_target_pairs={{0,3},{1,0},{2,1},{3,2},{4,7},{5,4},{6,5},{7,6},{8,11},{9,8},{10,9... | collective-permute-start | bytes 1179656 | tf_op jit(solution)/shard_map/ppermute | solution.py:47
  337.3 24.3 %copy-start.6 = (bf16[256,768]{1,0:T(8,128)(2,1)S(1)}, bf16[256,768]{1,0:T(8,128)(2,1)}, u32[]{:S(2)}) copy-start(bf16[256,768]{1,0:T(8,128)(2,1)} %get-tuple-element.208.refs_3_) | copy-start | bytes 1179652
  337.3 24.3 %copy-start.44 = (f32[256]{0:T(256)S(1)}, f32[256]{0:T(256)}, u32[]{:S(2)}) copy-start(f32[256]{0:T(256)} %get-tuple-element.285) | copy-start | bytes 3076
  337.4 17.5 %collective-permute-start.22 = (f32[4,768]{1,0:T(4,128)S(1)}, f32[4,768]{1,0:T(4,128)S(1)}, u32[]{:S(2)}, u32[]{:S(2)}) collective-permute-start(f32[4,768]{1,0:T(4,128)S(1)} %select_add_fusion), channel_id=1, source_target_pairs={{0,1},{1,0},{2,3},{3,2},{4,5},{5,4},{6,7},{7,6},{8,9},{9,8},{10,11... | collective-permute-start | bytes 36872 | tf_op jit(solution)/shard_map/ppermute | solution.py:387
  354.9 14.5 %collective-permute-start.25 = (bf16[768,576]{0,1:T(8,128)(2,1)S(1)}, bf16[768,576]{0,1:T(8,128)(2,1)}, u32[]{:S(2)}, u32[]{:S(2)}) collective-permute-start(bf16[768,576]{0,1:T(8,128)(2,1)S(1)} %copy-done.51), channel_id=1, source_target_pairs={{0,16},{1,17},{2,18},{3,19},{4,20},{5,21},{6,22},{7,23},{8,24},{9,... | collective-permute-start | bytes 2654216 | tf_op jit(solution)/shard_map/ppermute | solution.py:443
  356.2 7.1 %collective-permute-start.10 = (bf16[256,768]{1,0:T(8,128)(2,1)S(1)}, bf16[256,768]{1,0:T(8,128)(2,1)S(1)}, u32[]{:S(2)}, u32[]{:S(2)}) collective-permute-start(bf16[256,768]{1,0:T(8,128)(2,1)S(1)} %get-tuple-element.267), channel_id=1, source_target_pairs={{0,16},{16,0},{1,17},{17,1},{2,18},{18,2},{3,19},{19,3},{4,20},{20... | collective-permute-start | bytes 1179656 | tf_op jit(solution)/shard_map/ppermute | solution.py:400
  358.3 29.6 %collective-permute-start.26 = (bf16[768,768]{1,0:T(8,128)(2,1)}, bf16[768,768]{1,0:T(8,128)(2,1)}, u32[]{:S(2)}, u32[]{:S(2)}) collective-permute-start(bf16[768,768]{1,0:T(8,128)(2,1)} %get-tuple-element.319), channel_id=1, source_target_pairs={{16,0},{17,1},{18,2},{19,3},{20,4},{21,5},{22,6},{23,7},{24,8},{25... | collective-permute-start | bytes 3538952 | tf_op jit(solution)/shard_map/ppermute | solution.py:443
  361.3 4.3 collective-permute-start.23
  363.4 18.9 %collective-permute-start.24 = (bf16[768,576]{0,1:T(8,128)(2,1)}, bf16[768,576]{0,1:T(8,128)(2,1)}, u32[]{:S(2)}, u32[]{:S(2)}) collective-permute-start(bf16[768,576]{0,1:T(8,128)(2,1)} %get-tuple-element.315), channel_id=1, source_target_pairs={{16,0},{17,1},{18,2},{19,3},{20,4},{21,5},{22,6},{23,7},{24,8},{25... | collective-permute-start | bytes 2654216 | tf_op jit(solution)/shard_map/ppermute | solution.py:443
  365.6 5.3 %collective-permute-start.20 = (bf16[256,768]{1,0:T(8,128)(2,1)S(1)}, bf16[256,768]{1,0:T(8,128)(2,1)}, u32[]{:S(2)}, u32[]{:S(2)}) collective-permute-start(bf16[256,768]{1,0:T(8,128)(2,1)S(1)} %broadcast_select_fusion), channel_id=1, source_target_pairs={{0,16},{16,0},{1,17},{17,1},{2,18},{18,2},{3,19},{19,3},{4,20},{20... | collective-permute-start | bytes 1179656 | tf_op jit(solution)/shard_map/ppermute | solution.py:400
  369.4 24.7 %collective-permute-start.29 = (bf16[960,768]{1,0:T(8,128)(2,1)}, bf16[960,768]{1,0:T(8,128)(2,1)}, u32[]{:S(2)}, u32[]{:S(2)}) collective-permute-start(bf16[960,768]{1,0:T(8,128)(2,1)} %get-tuple-element.325), channel_id=1, source_target_pairs={{0,16},{1,17},{2,18},{3,19},{4,20},{5,21},{6,22},{7,23},{8,24},{9,... | collective-permute-start | bytes 4423688 | tf_op jit(solution)/shard_map/ppermute | solution.py:443
  370.9 23.3 %collective-permute-start.28 = (bf16[960,768]{1,0:T(8,128)(2,1)}, bf16[960,768]{1,0:T(8,128)(2,1)}, u32[]{:S(2)}, u32[]{:S(2)}) collective-permute-start(bf16[960,768]{1,0:T(8,128)(2,1)} %get-tuple-element.323), channel_id=1, source_target_pairs={{16,0},{17,1},{18,2},{19,3},{20,4},{21,5},{22,6},{23,7},{24,8},{25... | collective-permute-start | bytes 4423688 | tf_op jit(solution)/shard_map/ppermute | solution.py:443
  (60 other events, 317.2 us)
